TPU v7x, 32 devices: a whole 2x2x4 slice. The times are simulated.
32 devices in a mesh: groups: 2 (over x), corpus: 4 (over y, core), query: 4 (over z).
Axes of the slice: x: 2, y: 2, z: 4, core: 2. Of those that a mesh axis runs over, the one named last changes fastest.
Arguments:
- queries: bfloat16 [32, 32, 128], P(('groups', 'corpus', 'query')), parts along dimension 0, may hold values from -0.5 to 0.5
- passages: bfloat16 [4096, 180, 128], P(('groups', 'corpus', 'query')), parts along dimension 0, may hold values from -0.5 to 0.5
- token_lengths: int32 [4096], P('groups'), parts along dimension 0, may hold values from 19 to 180
- candidates: int32 [32, 256], P(('groups', 'corpus', 'query')), parts along dimension 0, may hold values from 0 to 2047, as said below
- passage_home: int32 [4096], P('groups'), parts along dimension 0, may hold values from 0 to 2047, as said below
Outputs:
- top_scores: float32 [32, 100], P(('groups', 'corpus', 'query')), parts along dimension 0
There are 2 independent parts, one for each index of `groups`. A program takes and returns all parts, laid end to end along the dimension named above; each array names one. Nothing has to cross between parts.
Inputs may be any that keep to these rules, and one draw needn't show every extreme that they name: A permutation of the stored rows; passage id c is stored on device passage_home[c] // 128 of corpus+query. The 256 candidates of a query are distinct; among the 256 candidates of one device's queries at most 32 are stored on any one device, and exactly 32 on some device.
All inputs are finite; a program needn't handle non-finite values.
Results may differ from a plain program's by a relative error of at most 0.0003.
Values may be sent and summed in bfloat16 or wider, within the bound.
A program may use at most 128 MiB of HBM per device.

v0:
```python
import jax
import jax.numpy as jnp
from jax import lax
from jax.sharding import PartitionSpec as P

TOPK = 100


def score_pairs(query_flat, block_flat, pair_lengths, query_tokens, token_slots, width):
    query_tok = query_flat.reshape(-1, query_tokens, width)
    blocks = block_flat.reshape(-1, token_slots, width)
    similar = jnp.einsum("nqd,npd->nqp", query_tok, blocks, preferred_element_type=jnp.float32)
    inside = jnp.arange(token_slots, dtype=jnp.int32)[None, None, :] < pair_lengths[:, None, None]
    return jnp.sum(jnp.max(jnp.where(inside, similar, -1e30), axis=2), axis=1)


def on_device(queries, passages, token_lengths, candidates, passage_home):
    shard_count = lax.axis_size(("corpus", "query"))
    query_count, cand_count = candidates.shape
    slab_rows = passages.shape[0]
    token_slots = passages.shape[1]
    width = passages.shape[2]
    query_tokens = queries.shape[1]
    flat_pass = passages.reshape(slab_rows, token_slots * width)
    flat_query = queries.reshape(query_count, query_tokens * width)
    capacity = max(2, 2 * query_count * cand_count // shard_count)
    flat_ids = candidates.reshape(-1)
    stored = passage_home[flat_ids]
    pair_lengths = token_lengths[flat_ids]
    target = stored // slab_rows
    offset = stored % slab_rows
    onehot = (target[:, None] == jnp.arange(shard_count, dtype=jnp.int32)[None, :]).astype(
        jnp.int32
    )
    ranked = jnp.sum(jnp.cumsum(onehot, axis=0) * onehot, axis=1) - 1
    position = target * capacity + ranked
    owner_query = jnp.arange(query_count * cand_count, dtype=jnp.int32) // cand_count
    total_slots = shard_count * capacity
    row_slots = (
        jnp.zeros((total_slots,), jnp.int32).at[position].set(offset).reshape(shard_count, capacity)
    )
    length_slots = (
        jnp.ones((total_slots,), jnp.int32)
        .at[position]
        .set(pair_lengths)
        .reshape(shard_count, capacity)
    )
    query_slots = jnp.zeros((total_slots,), jnp.int32).at[position].set(owner_query)
    query_tok = flat_query[query_slots].reshape(shard_count, capacity, query_tokens * width)
    tokens_in = lax.all_to_all(
        query_tok, ("corpus", "query"), split_axis=0, concat_axis=0, tiled=True
    )
    rows_in = lax.all_to_all(
        row_slots, ("corpus", "query"), split_axis=0, concat_axis=0, tiled=True
    )
    lengths_in = lax.all_to_all(
        length_slots, ("corpus", "query"), split_axis=0, concat_axis=0, tiled=True
    )
    item_count = rows_in.shape[1]
    blocks = flat_pass[rows_in.reshape(-1)]
    partial_value = score_pairs(
        tokens_in.reshape(-1, query_tokens * width),
        blocks,
        lengths_in.reshape(-1),
        query_tokens,
        token_slots,
        width,
    )
    returned = lax.all_to_all(
        partial_value.reshape(shard_count, item_count),
        ("corpus", "query"),
        split_axis=0,
        concat_axis=0,
        tiled=True,
    )
    scores = returned.reshape(-1)[position].reshape(query_count, cand_count)
    return lax.top_k(scores, TOPK)[0]


def solution(mesh):
    placed = (
        P(("groups", "corpus", "query"), None, None),
        P(("groups", "corpus", "query"), None, None),
        P("groups"),
        P(("groups", "corpus", "query"), None),
        P("groups"),
    )
    return jax.shard_map(
        on_device,
        mesh=mesh,
        in_specs=placed,
        out_specs=P(("groups", "corpus", "query"), None),
        check_vma=False,
    )
```

profile of v0, /device:TPU:1, one launch (start us, length us, event | category | flops | bytes accessed | tf_op | source)
XLA Modules:
  0.0 202.5 jit_solution(15678257151472394844)
XLA Ops:
  0.0 0.0 copy-start
  0.0 0.7 compare_select_fusion.2
  0.7 0.0 copy-done
  0.7 1.7 gather_fusion
  2.5 0.6 reduce-window.6
  3.1 0.2 slice_reduce_fusion
  3.3 0.1 fusion.1
  3.4 1.4 scatter_custom_fusion.1
  4.8 0.7 all_to_all.24
  5.5 7.4 %all-to-all-start.2 = ((s32[16,1,32]{2,1,0:T(1,128)}), s32[16,1,32]{2,1,0:T(1,128)S(1)}, u32[]{:S(2)}, u32[]{:S(2)}) async-start(s32[16,1,32]{2,1,0:T(1,128)} %all_to_all.24), calls=%async_computation.2 | async-start | bytes 16384 | tf_op jit(solution)/shard_map/all_to_all | solution.py:53
  12.9 1.9 gather_fusion.1
  14.8 1.4 scatter_custom_fusion
  16.2 0.1 all_to_all.21
  16.3 2.4 %all-to-all-done.2 = s32[16,1,32]{2,1,0:T(1,128)S(1)} async-done(((s32[16,1,32]{2,1,0:T(1,128)}), s32[16,1,32]{2,1,0:T(1,128)S(1)}, u32[]{:S(2)}, u32[]{:S(2)}) %all-to-all-start.2) | async-done | bytes 2080 | tf_op jit(solution)/shard_map/all_to_all | solution.py:53
  18.7 9.2 %all_to_all.32 = s32[16,1,32]{2,1,0:T(1,128)S(1)} all-to-all(s32[16,1,32]{2,1,0:T(1,128)S(1)} %all_to_all.21), channel_id=1, replica_groups=mesh['groups'=2,'corpus'=4,'query'=4] {'corpus','query'}, dimensions={0} | all-to-all | bytes 4096 | tf_op jit(solution)/shard_map/all_to_all | solution.py:56
  27.9 3.2 %broadcast.213 = bf16[16,32,4096]{2,1,0:T(8,128)(2,1)} broadcast(bf16[4096]{0:T(1024)(128)(2,1)} %bitcast.43), dimensions={2} | broadcast | bytes 4202496 | tf_op jit(solution)/shard_map/reshape | solution.py:49
  31.1 5.0 %all-to-all-start.1 = ((bf16[16,32,4096]{2,1,0:T(8,128)(2,1)}), bf16[16,32,4096]{2,1,0:T(8,128)(2,1)}, u32[]{:S(2)}, u32[]{:S(2)}) async-start(bf16[16,32,4096]{2,1,0:T(8,128)(2,1)} %broadcast.213), calls=%async_computation.1 | async-start | bytes 8388608 | tf_op jit(solution)/shard_map/all_to_all | solution.py:50
  36.0 8.4 %copy.18 = bf16[128,180,128]{0,2,1:T(8,128)(2,1)} copy(bf16[128,180,128]{2,0,1:T(8,128)(2,1)} %param.6) | data formatting | bytes 11796480 | tf_op args[1]
  44.5 8.4 %copy.19 = bf16[128,23040]{1,0:T(8,128)(2,1)} copy(bf16[128,23040]{0,1:T(8,128)(2,1)} %bitcast.40) | data formatting | bytes 11796480 | tf_op jit(solution)/shard_map/reshape | solution.py:24
  52.9 0.5 broadcast.280
  53.4 0.7 reduce.12
  54.1 0.1 reshape.216
  54.2 43.8 %gather_fusion.2 = bf16[512,23040]{1,0:T(8,128)(2,1)} fusion(bf16[128,23040]{1,0:T(8,128)(2,1)} %copy.19, s32[1024]{0:T(1024)S(1)} %pad_clamp_fusion.1), kind=kCustom, calls=%fused_computation.2 | custom fusion | bytes 47187968 | tf_op jit(solution)/shard_map/gather | solution.py:60
  98.0 30.6 %copy.20 = bf16[512,23040]{0,1:T(8,128)(2,1)} copy(bf16[512,23040]{1,0:T(8,128)(2,1)} %gather_fusion.2) | data formatting | bytes 47185920 | tf_op jit(solution)/shard_map/gather | solution.py:60
  128.6 31.6 %copy.21 = bf16[512,180,128]{2,1,0:T(8,128)(2,1)} copy(bf16[512,180,128]{0,2,1:T(8,128)(2,1)} %bitcast.39) | data formatting | bytes 47185920 | tf_op jit(solution)/shard_map/reshape | solution.py:11
  160.2 0.7 reduce.13
  160.8 0.1 lt.66
  160.9 0.1 iota_compare_fusion
  161.1 0.0 all-to-all-done.1
  161.1 3.4 %copy.25 = bf16[64,8,32,128]{3,2,1,0:T(8,128)(2,1)S(1)} copy(bf16[64,8,32,128]{3,1,2,0:T(8,128)(2,1)} %bitcast.15) | data formatting | bytes 8388608
  164.5 0.0 copy-start.1
  164.5 19.0 %select_reduce_fusion = f32[512,32]{1,0:T(8,128)S(1)} fusion(bf16[512,180,128]{2,1,0:T(8,128)(2,1)} %copy.21, bf16[512,32,128]{2,1,0:T(8,128)(2,1)S(1)} %bitcast.41, pred[512,180]{1,0:T(8,128)(4,1)S(1)} %iota_compare_fusion), kind=kOutput, calls=%fused_computation.6 | convolution fusion | flops 760856576 | bytes 27944960 | tf_op jit(solution)/shard_map/nqd,npd->nqp/dot_general | solution.py:12
  183.5 0.2 reduce_sum.19
  183.7 0.7 all_to_all.26
  184.4 6.1 %all-to-all-start.3 = ((f32[16,1,32]{2,1,0:T(1,128)}), f32[16,1,32]{2,1,0:T(1,128)S(1)}, u32[]{:S(2)}, u32[]{:S(2)}) async-start(f32[16,1,32]{2,1,0:T(1,128)} %all_to_all.26), calls=%async_computation.3 | async-start | bytes 16384 | tf_op jit(solution)/shard_map/all_to_all | solution.py:69
  190.4 5.8 %all-to-all-done.3 = f32[16,1,32]{2,1,0:T(1,128)S(1)} async-done(((f32[16,1,32]{2,1,0:T(1,128)}), f32[16,1,32]{2,1,0:T(1,128)S(1)}, u32[]{:S(2)}, u32[]{:S(2)}) %all-to-all-start.3) | async-done | bytes 2080 | tf_op jit(solution)/shard_map/all_to_all | solution.py:69
  196.2 0.5 broadcast.282
  196.7 0.7 reduce.14
  197.4 0.1 reshape.218
  197.5 1.9 gather_fusion.3
  199.4 3.1 %sort_prefixfusion = f32[1,100]{1,0:T(1,128)} fusion(f32[1,256]{1,0:T(1,128)S(1)} %bitcast.50), kind=kCustom, calls=%top_k.9.sort_prefix | custom fusion | flops 2048 | bytes 1424 | tf_op jit(solution)/shard_map/top_k | solution.py:77
  202.5 0.0 copy-done.1
  (11 shorter events, 0.1 us)
Async XLA Ops:
  0.0 0.7 copy-start
  5.5 13.1 %all-to-all-start.2 = ((s32[16,1,32]{2,1,0:T(1,128)}), s32[16,1,32]{2,1,0:T(1,128)S(1)}, u32[]{:S(2)}, u32[]{:S(2)}) async-start(s32[16,1,32]{2,1,0:T(1,128)} %all_to_all.24), calls=%async_computation.2 | async-start | bytes 16384 | tf_op jit(solution)/shard_map/all_to_all | solution.py:53
  31.1 130.0 %all-to-all-start.1 = ((bf16[16,32,4096]{2,1,0:T(8,128)(2,1)}), bf16[16,32,4096]{2,1,0:T(8,128)(2,1)}, u32[]{:S(2)}, u32[]{:S(2)}) async-start(bf16[16,32,4096]{2,1,0:T(8,128)(2,1)} %broadcast.213), calls=%async_computation.1 | async-start | bytes 8388608 | tf_op jit(solution)/shard_map/all_to_all | solution.py:50
  164.5 38.0 %copy-start.1 = (s32[2048]{0:T(1024)S(1)}, s32[2048]{0:T(1024)}, u32[]{:S(2)}) copy-start(s32[2048]{0:T(1024)} %param.9) | copy-start | bytes 24580
  184.4 11.9 %all-to-all-start.3 = ((f32[16,1,32]{2,1,0:T(1,128)}), f32[16,1,32]{2,1,0:T(1,128)S(1)}, u32[]{:S(2)}, u32[]{:S(2)}) async-start(f32[16,1,32]{2,1,0:T(1,128)} %all_to_all.26), calls=%async_computation.3 | async-start | bytes 16384 | tf_op jit(solution)/shard_map/all_to_all | solution.py:69
where the time goes:
time: 206 us; the launch traced here: 202 us
  local copies, waits for them, and re-layouts  141 us (68%)
  matrix products  19 us (9%)
  starting transfers between devices  18.4 us (9%)
  blocking collectives  9.24 us (4%)
  waiting for transfers between devices  8.15 us (4%)
  other arithmetic  6.85 us (3%)
    gather x2, local copies, waits for them, and re-layouts, on_device(): blocks = flat_pass[rows_in.reshape(-1)]  74.4 us
    reshape x1, local copies, waits for them, and re-layouts, score_pairs(): blocks = block_flat.reshape(-1, token_slots, width)  31.6 us
    dot_general x1, matrix products, score_pairs(): jnp.einsum('nqd,npd->nqp', query_tok, blocks, preferred_element_type=jnp....  19 us
    unnamed x6, local copies, waits for them, and re-layouts  11.9 us
    all_to_all x1, blocking collectives, on_device(): lax.all_to_all(length_slots, ('corpus', 'query'), split_axis=0, concat_ax...  9.24 us
    reshape x1, local copies, waits for them, and re-layouts, on_device(): flat_pass = passages.reshape(slab_rows, token_slots * width)  8.41 us
    all_to_all x1, starting transfers between devices, on_device(): lax.all_to_all(row_slots, ('corpus', 'query'), split_axis=0, concat_axis=...  7.35 us
    all_to_all x1, starting transfers between devices, on_device(): lax.all_to_all(partial_value.reshape(shard_count, item_count), ('corpus',...  6.06 us
  transfers between devices with their start and end apart: 3, of which 2 were waited for; matrix products, arithmetic and copies ran while one was open for 63% of the time, Pallas kernels for 0%

commit v1 on v0

v1 whole, which is shorter than its diff:
```python
import functools

import jax
import jax.numpy as jnp
from jax import lax
from jax.experimental import pallas as pl
from jax.experimental.pallas import tpu as pltpu
from jax.sharding import PartitionSpec as P

TOPK = 100
LANES = 128
MESH = pl.DeviceIdType.MESH
F32, BF16, I32 = jnp.float32, jnp.bfloat16, jnp.int32


def split3(x):
    hi = x.astype(BF16)
    rest = x - hi.astype(F32)
    mid = rest.astype(BF16)
    return hi, mid, (rest - mid.astype(F32)).astype(BF16)


def dot_nt(a, b):
    return lax.dot_general(a, b, (((1,), (1,)), ((), ())), preferred_element_type=F32)


def kernel(
    shards, inner, tile, chunk, band,
    q_ref, pass_ref, len_ref, cand_ref, home_ref, out_ref,
    slab, qbuf, lens, best, sent, got, where_row,
    load_sem, qs_sem, qr_sem, ss_sem, sr_sem,
):
    slots, slab_rows, width = slab.shape
    tokens = qbuf.shape[1]
    me = lax.axis_index("corpus") * inner + lax.axis_index("query")
    chunks = slots // chunk

    def load(c):
        part = pl.ds(c * chunk, chunk)
        return pltpu.make_async_copy(pass_ref.at[part], slab.at[part], load_sem.at[c])

    for c in range(chunks):
        load(c).start()

    def peer(d):
        p = lax.rem(me + d, shards)
        return p, {"corpus": p // inner, "query": lax.rem(p, inner)}

    barrier = pltpu.get_barrier_semaphore()

    def greet(d, carry):
        pl.semaphore_signal(barrier, inc=1, device_id=peer(d)[1], device_id_type=MESH)
        return carry

    lax.fori_loop(1, shards, greet, 0)
    pl.semaphore_wait(barrier, shards - 1)

    def query_copy(slot, sem_s, device):
        return pltpu.make_async_remote_copy(
            src_ref=q_ref, dst_ref=qbuf.at[pl.ds(slot, 1)],
            send_sem=qs_sem.at[sem_s], recv_sem=qr_sem.at[slot],
            device_id=device, device_id_type=MESH,
        )

    def score_copy(row, slot, device):
        return pltpu.make_async_remote_copy(
            src_ref=sent.at[row], dst_ref=got.at[slot],
            send_sem=ss_sem.at[row], recv_sem=sr_sem.at[slot],
            device_id=device, device_id_type=MESH,
        )

    def send_query(d, carry):
        p, device = peer(d)
        query_copy(me, p, device).start()
        return carry

    lax.fori_loop(1, shards, send_query, 0)
    qbuf[pl.ds(me, 1)] = q_ref[...]

    stored = lax.broadcasted_iota(I32, (slab_rows, LANES), 0) + me * slab_rows
    picked = jnp.zeros((slab_rows, LANES), I32)
    for b in range(home_ref.shape[0]):
        hit = home_ref[b : b + 1, :] == stored
        picked = jnp.where(hit, len_ref[b : b + 1, :], picked)
    ones = jnp.ones((LANES, LANES), BF16)
    lens[...] = jnp.dot(
        picked.astype(F32).astype(BF16), ones, preferred_element_type=F32
    ).astype(I32)

    count = cand_ref.shape[1]
    cand = cand_ref[...]
    low = lax.broadcasted_iota(I32, (LANES, count), 0) == lax.rem(cand, LANES)
    low = jnp.where(low, 1.0, 0.0).astype(BF16)
    home = home_ref[...]
    blocks = home.shape[0]
    high = lax.broadcasted_iota(I32, (blocks, count), 0) == cand // LANES
    for k, part in enumerate((home // slab_rows, lax.rem(home, slab_rows))):
        table = jnp.dot(part.astype(F32).astype(BF16), low, preferred_element_type=F32)
        where_row[k : k + 1, :] = jnp.sum(
            jnp.where(high, table, 0.0), axis=0, keepdims=True
        ).astype(I32)

    def wait_load(c, carry):
        load(c).wait()
        return carry

    lax.fori_loop(0, chunks, wait_load, 0)

    columns = tile * tokens
    tiles = shards // tile
    group = lax.broadcasted_iota(I32, (tile, columns), 0)
    member = lax.broadcasted_iota(I32, (tile, columns), 1) // tokens
    adder = jnp.where(group == member, 1.0, 0.0).astype(BF16)

    def one_tile(b, carry):
        t = lax.rem(me // tile + b, tiles)

        def wait_query(i, c):
            p = t * tile + i

            @pl.when(p != me)
            def _():
                query_copy(p, p, {"query": lax.axis_index("query")}).wait_recv()

            return c

        lax.fori_loop(0, tile, wait_query, 0)
        query = qbuf[pl.ds(t * tile, tile)].reshape(columns, width)

        for r in range(0, slab_rows, band):
            live = lens[r : r + band, :]

            def some_slots(g, top):
                block = slab[pl.ds(g * chunk, chunk), r : r + band, :]
                similar = dot_nt(block.reshape(chunk * band, width), query)
                for u in range(chunk):
                    inside = live > g * chunk + u
                    row = similar[u * band : (u + 1) * band]
                    top = tuple(
                        jnp.maximum(
                            old,
                            jnp.where(inside, row[:, k * LANES : (k + 1) * LANES], -1e30),
                        )
                        for k, old in enumerate(top)
                    )
                return top

            start = tuple(
                jnp.full((band, LANES), -1e30, F32) for _ in range(columns // LANES)
            )
            top = lax.fori_loop(0, chunks, some_slots, start)
            best[r : r + band, :] = jnp.concatenate(top, axis=1)
        hi, mid, lo = split3(best[...])
        scores = dot_nt(adder, lo) + dot_nt(adder, mid) + dot_nt(adder, hi)
        for i in range(tile):
            p = t * tile + i
            sent[pl.ds(p, 1)] = scores[i : i + 1].reshape(1, 1, slab_rows)

            @pl.when(p != me)
            def _():
                device = {"corpus": p // inner, "query": lax.rem(p, inner)}
                score_copy(p, me, device).start()

            @pl.when(p == me)
            def _():
                got[pl.ds(p, 1)] = scores[i : i + 1].reshape(1, 1, slab_rows)

        return carry

    lax.fori_loop(0, tiles, one_tile, 0)

    def wait_scores(d, carry):
        p, device = peer(d)
        score_copy(p, p, device).wait_recv()
        return carry

    lax.fori_loop(1, shards, wait_scores, 0)
    table = got[...].reshape(shards, slab_rows)
    offset = lax.broadcasted_iota(I32, (slab_rows, count), 0) == where_row[1:2, :]
    offset = jnp.where(offset, 1.0, 0.0).astype(BF16)
    hi, mid, lo = split3(table)
    dot = functools.partial(jnp.dot, preferred_element_type=F32)
    found = (dot(hi, offset) + dot(mid, offset)) + dot(lo, offset)
    shard = lax.broadcasted_iota(I32, (shards, count), 0) == where_row[0:1, :]
    score = jnp.sum(jnp.where(shard, found, 0.0), axis=0, keepdims=True)

    down = jnp.transpose(jnp.broadcast_to(score, (LANES, count)))
    mine = lax.broadcasted_iota(I32, (count, LANES), 0)
    rank = jnp.zeros((count, LANES), F32)
    for k in range(0, count, LANES):
        other = lax.broadcasted_iota(I32, (count, LANES), 1) + k
        across = score[:, k : k + LANES]
        ahead = (across > down) | ((across == down) & (other < mine))
        rank += jnp.where(ahead, 1.0, 0.0)
    rank = jnp.dot(rank.astype(BF16), ones, preferred_element_type=F32)
    slot = lax.broadcasted_iota(I32, (count, LANES), 1).astype(F32)
    ranked = jnp.sum(jnp.where(rank == slot, down, 0.0), axis=0, keepdims=True)
    out_ref[...] = ranked[:, : out_ref.shape[1]]

    def wait_sends(d, carry):
        p, device = peer(d)
        query_copy(p, p, device).wait_send()
        score_copy(p, p, device).wait_send()
        return carry

    lax.fori_loop(1, shards, wait_sends, 0)


def on_device(queries, passages, token_lengths, candidates, passage_home):
    inner = lax.axis_size("query")
    shards = lax.axis_size("corpus") * inner
    slab_rows, slots, width = passages.shape
    tokens = queries.shape[1]
    count = candidates.shape[1]
    tile = max(1, 256 // tokens)
    while shards % tile:
        tile -= 1
    chunk = next(c for c in range(12, 0, -1) if slots % c == 0)
    band = 32
    by_slot = jnp.transpose(passages, (1, 0, 2))
    vmem = pl.BlockSpec(memory_space=pltpu.VMEM)
    return pl.pallas_call(
        functools.partial(kernel, shards, inner, tile, chunk, band),
        out_shape=jax.ShapeDtypeStruct((1, TOPK), F32),
        in_specs=[vmem, pl.BlockSpec(memory_space=pltpu.HBM), vmem, vmem, vmem],
        out_specs=vmem,
        scratch_shapes=[
            pltpu.VMEM(by_slot.shape, BF16),
            pltpu.VMEM((shards, tokens, width), BF16),
            pltpu.VMEM((slab_rows, LANES), I32),
            pltpu.VMEM((slab_rows, tile * tokens), F32),
            pltpu.VMEM((shards, 1, slab_rows), F32),
            pltpu.VMEM((shards, 1, slab_rows), F32),
            pltpu.VMEM((8, count), I32),
            pltpu.SemaphoreType.DMA((slots // chunk,)),
            pltpu.SemaphoreType.DMA((shards,)),
            pltpu.SemaphoreType.DMA((shards,)),
            pltpu.SemaphoreType.DMA((shards,)),
            pltpu.SemaphoreType.DMA((shards,)),
        ],
        compiler_params=pltpu.CompilerParams(
            collective_id=0, has_side_effects=True, vmem_limit_bytes=32 * 1024 * 1024
        ),
    )(
        queries,
        by_slot,
        token_lengths.reshape(-1, LANES),
        candidates,
        passage_home.reshape(-1, LANES),
    )


def solution(mesh):
    placed = (
        P(("groups", "corpus", "query"), None, None),
        P(("groups", "corpus", "query"), None, None),
        P("groups"),
        P(("groups", "corpus", "query"), None),
        P("groups"),
    )
    return jax.shard_map(
        on_device,
        mesh=mesh,
        in_specs=placed,
        out_specs=P(("groups", "corpus", "query"), None),
        check_vma=False,
    )
```

time: 206 us -> 51.5 us (0.25); the launches traced: 202 us -> 50.6 us
  local copies, waits for them, and re-layouts: 141 us -> 5.95 us
  Pallas kernels: 0 us -> 44.6 us
  matrix products: 19 us -> 0 us
  starting transfers between devices: 18.4 us -> 0 us
  blocking collectives: 9.24 us -> 0 us
  waiting for transfers between devices: 8.15 us -> 0 us
  other arithmetic: 6.85 us -> 0 us
    gather x5 -> x0, local copies, waits for them, and re-layouts: 80 us -> none  [the longest x2 74.4 us: on_device(): blocks = flat_pass[rows_in.reshape(-1)]]
    pallas_call x0 -> x1, Pallas kernels: none -> 44.6 us  [on_device(): pl.pallas_call(functools.partial(kernel, shards, inner, tile, chunk, band...]
    reshape x5 -> x0, local copies, waits for them, and re-layouts: 43.3 us -> none  [the longest x1 31.6 us: score_pairs(): blocks = block_flat.reshape(-1, token_slots, width)]
    dot_general x1 -> x0, matrix products: 19 us -> none  [score_pairs(): jnp.einsum('nqd,npd->nqp', query_tok, blocks, preferred_element_type=jnp....]
    all_to_all x3 -> x0, starting transfers between devices: 18.4 us -> none  [the longest x1 7.35 us: on_device(): lax.all_to_all(row_slots, ('corpus', 'query'), split_axis=0, concat_axis=...]
    all_to_all x1 -> x0, blocking collectives: 9.24 us -> none  [on_device(): lax.all_to_all(length_slots, ('corpus', 'query'), split_axis=0, concat_ax...]
    all_to_all x3 -> x0, waiting for transfers between devices: 8.15 us -> none  [the longest x1 5.78 us: on_device(): lax.all_to_all(partial_value.reshape(shard_count, item_count), ('corpus',...]
    unnamed x6 -> x11, local copies, waits for them, and re-layouts: 11.9 us -> 5.95 us
  transfers between devices with their start and end apart: 3 -> 0, of which waited for: 2 -> 0; matrix products, arithmetic and copies ran while one was open for 63% -> 0% of each run, Pallas kernels for 0% -> 0%
where the time goes in v1:
time: 51.5 us; the launch traced here: 50.6 us
  Pallas kernels  44.6 us (87%)
  local copies, waits for them, and re-layouts  5.95 us (12%)
    pallas_call x1, Pallas kernels, on_device(): pl.pallas_call(functools.partial(kernel, shards, inner, tile, chunk, band...  44.6 us
    unnamed x11, local copies, waits for them, and re-layouts  5.95 us

profile of v1, /device:TPU:1, one launch (start us, length us, event | category | flops | bytes accessed | tf_op | source)
XLA Modules:
  0.0 50.6 jit_solution(12942249045271990837)
XLA Ops:
  0.0 0.0 copy-start
  0.0 2.7 %copy-done = bf16[128,180,128]{2,0,1:T(8,128)(2,1)S(1)} copy-done((bf16[128,180,128]{2,0,1:T(8,128)(2,1)S(1)}, bf16[128,180,128]{2,0,1:T(8,128)(2,1)}, u32[]{:S(2)}) %copy-start) | copy-done | bytes 5898264
  2.7 0.0 copy-start.1
  2.7 0.7 %copy-done.1 = bf16[1,32,128]{2,1,0:T(8,128)(2,1)S(1)} copy-done((bf16[1,32,128]{2,1,0:T(8,128)(2,1)S(1)}, bf16[1,32,128]{2,1,0:T(8,128)(2,1)}, u32[]{:S(2)}) %copy-start.1) | copy-done | bytes 8216
  3.4 0.0 copy-start.2
  3.4 0.7 %copy-done.2 = s32[2048]{0:T(1024)S(1)} copy-done((s32[2048]{0:T(1024)S(1)}, s32[2048]{0:T(1024)}, u32[]{:S(2)}) %copy-start.2) | copy-done | bytes 8216
  4.1 0.0 copy-start.3
  4.1 0.7 %copy-done.3 = s32[2048]{0:T(1024)S(1)} copy-done((s32[2048]{0:T(1024)S(1)}, s32[2048]{0:T(1024)}, u32[]{:S(2)}) %copy-start.3) | copy-done | bytes 8216
  4.8 0.0 copy-start.4
  4.8 0.7 %copy-done.4 = s32[1,256]{1,0:T(1,128)S(1)} copy-done((s32[1,256]{1,0:T(1,128)S(1)}, s32[1,256]{1,0:T(1,128)}, u32[]{:S(2)}) %copy-start.4) | copy-done | bytes 1048
  5.4 44.6 %shard_map.55 = f32[1,100]{1,0:T(1,128)S(1)} custom-call(bf16[1,32,128]{2,1,0:T(8,128)(2,1)S(1)} %copy-done.1, bf16[180,128,128]{2,1,0:T(8,128)(2,1)S(1)} %bitcast.3, s32[16,128]{1,0:T(8,128)S(1)} %bitcast.4, s32[1,256]{1,0:T(1,128)S(1)} %copy-done.4, s32[16,128]{1,0:T(8,128)S(1)} %bitcast.5), custom_call_target="tpu_custom_call" | custom-call | tf_op jit(solution)/shard_map/pallas_call | solution.py:222
  50.1 0.5 %copy.7 = f32[1,100]{1,0:T(1,128)} copy(f32[1,100]{1,0:T(1,128)S(1)} %shard_map.55) | data formatting | bytes 800
Async XLA Ops:
  0.0 2.7 %copy-start = (bf16[128,180,128]{2,0,1:T(8,128)(2,1)S(1)}, bf16[128,180,128]{2,0,1:T(8,128)(2,1)}, u32[]{:S(2)}) copy-start(bf16[128,180,128]{2,0,1:T(8,128)(2,1)} %param.6) | copy-start | bytes 17694724
  2.7 0.7 %copy-start.1 = (bf16[1,32,128]{2,1,0:T(8,128)(2,1)S(1)}, bf16[1,32,128]{2,1,0:T(8,128)(2,1)}, u32[]{:S(2)}) copy-start(bf16[1,32,128]{2,1,0:T(8,128)(2,1)} %q_ref.1) | copy-start | bytes 24580
  3.4 0.7 %copy-start.2 = (s32[2048]{0:T(1024)S(1)}, s32[2048]{0:T(1024)}, u32[]{:S(2)}) copy-start(s32[2048]{0:T(1024)} %param.7) | copy-start | bytes 24580
  4.1 0.7 %copy-start.3 = (s32[2048]{0:T(1024)S(1)}, s32[2048]{0:T(1024)}, u32[]{:S(2)}) copy-start(s32[2048]{0:T(1024)} %param.9) | copy-start | bytes 24580
  4.8 0.7 %copy-start.4 = (s32[1,256]{1,0:T(1,128)S(1)}, s32[1,256]{1,0:T(1,128)}, u32[]{:S(2)}) copy-start(s32[1,256]{1,0:T(1,128)} %cand_ref.1) | copy-start | bytes 3076

commit v2 on v1

--- a/solution.py
+++ b/solution.py
@@ -9,6 +9,7 @@
 
 TOPK = 100
 LANES = 128
+CHUNK, BAND, COLUMNS = 20, 128, 256
 MESH = pl.DeviceIdType.MESH
 F32, BF16, I32 = jnp.float32, jnp.bfloat16, jnp.int32
 
@@ -26,9 +27,9 @@
 
 def kernel(
     shards, inner, tile, chunk, band,
-    q_ref, pass_ref, len_ref, cand_ref, home_ref, out_ref,
-    slab, qbuf, lens, best, sent, got, where_row,
-    load_sem, qs_sem, qr_sem, ss_sem, sr_sem,
+    q_ref, pass_ref, len_hbm, cand_hbm, home_hbm, out_ref,
+    len_ref, cand_ref, home_ref, slab, query_t, qbuf, lens, best, sent, got, where_row,
+    small_sem, load_sem, qs_sem, qr_sem, ss_sem, sr_sem,
 ):
     slots, slab_rows, width = slab.shape
     tokens = qbuf.shape[1]
@@ -39,9 +40,6 @@
         part = pl.ds(c * chunk, chunk)
         return pltpu.make_async_copy(pass_ref.at[part], slab.at[part], load_sem.at[c])
 
-    for c in range(chunks):
-        load(c).start()
-
     def peer(d):
         p = lax.rem(me + d, shards)
         return p, {"corpus": p // inner, "query": lax.rem(p, inner)}
@@ -53,6 +51,21 @@
         return carry
 
     lax.fori_loop(1, shards, greet, 0)
+    small = [
+        pltpu.make_async_copy(src, dst, small_sem.at[k])
+        for k, (src, dst) in enumerate(
+            (
+                (home_hbm, home_ref),
+                (len_hbm, len_ref),
+                (cand_hbm, cand_ref),
+                (q_ref, qbuf.at[pl.ds(me, 1)]),
+            )
+        )
+    ]
+    for copy in small:
+        copy.start()
+    for c in range(chunks):
+        load(c).start()
     pl.semaphore_wait(barrier, shards - 1)
 
     def query_copy(slot, sem_s, device):
@@ -75,7 +88,8 @@
         return carry
 
     lax.fori_loop(1, shards, send_query, 0)
-    qbuf[pl.ds(me, 1)] = q_ref[...]
+    for copy in small:
+        copy.wait()
 
     stored = lax.broadcasted_iota(I32, (slab_rows, LANES), 0) + me * slab_rows
     picked = jnp.zeros((slab_rows, LANES), I32)
@@ -125,14 +139,17 @@
             return c
 
         lax.fori_loop(0, tile, wait_query, 0)
-        query = qbuf[pl.ds(t * tile, tile)].reshape(columns, width)
+        query_t[...] = qbuf[pl.ds(t * tile, tile)].reshape(columns, width).T
 
         for r in range(0, slab_rows, band):
             live = lens[r : r + band, :]
 
             def some_slots(g, top):
                 block = slab[pl.ds(g * chunk, chunk), r : r + band, :]
-                similar = dot_nt(block.reshape(chunk * band, width), query)
+                similar = jnp.dot(
+                    block.reshape(chunk * band, width), query_t[...],
+                    preferred_element_type=F32,
+                )
                 for u in range(chunk):
                     inside = live > g * chunk + u
                     row = similar[u * band : (u + 1) * band]
@@ -212,26 +229,31 @@
     slab_rows, slots, width = passages.shape
     tokens = queries.shape[1]
     count = candidates.shape[1]
-    tile = max(1, 256 // tokens)
+    tile = max(1, COLUMNS // tokens)
     while shards % tile:
         tile -= 1
-    chunk = next(c for c in range(12, 0, -1) if slots % c == 0)
-    band = 32
+    chunk = next(c for c in range(CHUNK, 0, -1) if slots % c == 0)
+    band = BAND if slab_rows % BAND == 0 else slab_rows
     by_slot = jnp.transpose(passages, (1, 0, 2))
     vmem = pl.BlockSpec(memory_space=pltpu.VMEM)
     return pl.pallas_call(
         functools.partial(kernel, shards, inner, tile, chunk, band),
         out_shape=jax.ShapeDtypeStruct((1, TOPK), F32),
-        in_specs=[vmem, pl.BlockSpec(memory_space=pltpu.HBM), vmem, vmem, vmem],
+        in_specs=[pl.BlockSpec(memory_space=pltpu.HBM)] * 5,
         out_specs=vmem,
         scratch_shapes=[
+            pltpu.VMEM((len(token_lengths) // LANES, LANES), I32),
+            pltpu.VMEM(candidates.shape, I32),
+            pltpu.VMEM((len(passage_home) // LANES, LANES), I32),
             pltpu.VMEM(by_slot.shape, BF16),
+            pltpu.VMEM((width, tile * tokens), BF16),
             pltpu.VMEM((shards, tokens, width), BF16),
             pltpu.VMEM((slab_rows, LANES), I32),
             pltpu.VMEM((slab_rows, tile * tokens), F32),
             pltpu.VMEM((shards, 1, slab_rows), F32),
             pltpu.VMEM((shards, 1, slab_rows), F32),
             pltpu.VMEM((8, count), I32),
+            pltpu.SemaphoreType.DMA((4,)),
             pltpu.SemaphoreType.DMA((slots // chunk,)),
             pltpu.SemaphoreType.DMA((shards,)),
             pltpu.SemaphoreType.DMA((shards,)),
@@ -239,7 +261,7 @@
             pltpu.SemaphoreType.DMA((shards,)),
         ],
         compiler_params=pltpu.CompilerParams(
-            collective_id=0, has_side_effects=True, vmem_limit_bytes=32 * 1024 * 1024
+            collective_id=0, has_side_effects=True, vmem_limit_bytes=56 * 1024 * 1024
         ),
     )(
         queries,

time: 51.5 us -> 26.6 us (0.52)
  the two profiles are of different devices: /device:TPU:1 before, /device:TPU:0 now
where the time goes in v2:
time: 26.6 us; the launch traced here: 26.4 us
  Pallas kernels  25.2 us (95%)
  local copies, waits for them, and re-layouts  1.19 us (4%)
    pallas_call x1, Pallas kernels, on_device(): pl.pallas_call(functools.partial(kernel, shards, inner, tile, chunk, band...  25.2 us
    unnamed x1, local copies, waits for them, and re-layouts  1.19 us

profile of v2, /device:TPU:0, one launch (start us, length us, event | category | flops | bytes accessed | tf_op | source)
XLA Modules:
  0.0 26.4 jit_solution(15942136636999950101)
XLA Ops:
  0.0 25.2 %shard_map.55 = f32[1,100]{1,0:T(1,128)} custom-call(bf16[1,32,128]{2,1,0:T(8,128)(2,1)} %q_ref.1, bf16[180,128,128]{2,1,0:T(8,128)(2,1)} %bitcast.3, s32[16,128]{1,0:T(8,128)} %bitcast.4, s32[1,256]{1,0:T(1,128)} %cand_hbm.1, s32[16,128]{1,0:T(8,128)} %bitcast.5), custom_call_target="tpu_custom_call" | custom-call | tf_op jit(solution)/shard_map/pallas_call | solution.py:239
  25.2 1.2 %copy.7 = f32[1,100]{1,0:T(1,128)} copy(f32[1,100]{1,0:T(1,128)} %shard_map.55) | data formatting | bytes 800

commit v3 on v2

--- a/solution.py
+++ b/solution.py
@@ -29,11 +29,22 @@
     shards, inner, tile, chunk, band,
     q_ref, pass_ref, len_hbm, cand_hbm, home_hbm, out_ref,
     len_ref, cand_ref, home_ref, slab, query_t, qbuf, lens, best, sent, got, where_row,
-    small_sem, load_sem, qs_sem, qr_sem, ss_sem, sr_sem,
+    small_sem, load_sem, qs_sem, qr_sem, ps_sem, pr_sem, ss_sem, sr_sem,
 ):
     slots, slab_rows, width = slab.shape
     tokens = qbuf.shape[1]
-    me = lax.axis_index("corpus") * inner + lax.axis_index("query")
+    mesh_me = lax.axis_index("corpus") * inner + lax.axis_index("query")
+    half = shards // 2
+    plane = lax.rem(lax.axis_index("corpus"), 2)
+    spot = (lax.axis_index("corpus") // 2) * inner + lax.axis_index("query")
+    me = plane * half + spot
+
+    def device_of(p):
+        rest = lax.rem(p, half)
+        corpus = (rest // inner) * 2 + p // half
+        query = lax.rem(rest, inner)
+        return corpus * inner + query, {"corpus": corpus, "query": query}
+
     chunks = slots // chunk
 
     def load(c):
@@ -42,12 +53,12 @@
 
     def peer(d):
         p = lax.rem(me + d, shards)
-        return p, {"corpus": p // inner, "query": lax.rem(p, inner)}
+        return p, *device_of(p)
 
     barrier = pltpu.get_barrier_semaphore()
 
     def greet(d, carry):
-        pl.semaphore_signal(barrier, inc=1, device_id=peer(d)[1], device_id_type=MESH)
+        pl.semaphore_signal(barrier, inc=1, device_id=peer(d)[2], device_id_type=MESH)
         return carry
 
     lax.fori_loop(1, shards, greet, 0)
@@ -82,16 +93,24 @@
             device_id=device, device_id_type=MESH,
         )
 
+    def plane_copy(which):
+        part = pl.ds(which * half, half)
+        return pltpu.make_async_remote_copy(
+            src_ref=qbuf.at[part], dst_ref=qbuf.at[part],
+            send_sem=ps_sem, recv_sem=pr_sem,
+            device_id=device_of((1 - plane) * half + spot)[1], device_id_type=MESH,
+        )
+
     def send_query(d, carry):
-        p, device = peer(d)
-        query_copy(me, p, device).start()
-        return carry
-
-    lax.fori_loop(1, shards, send_query, 0)
+        p = plane * half + lax.rem(spot + d, half)
+        query_copy(me, p, device_of(p)[1]).start()
+        return carry
+
+    lax.fori_loop(1, half, send_query, 0)
     for copy in small:
         copy.wait()
 
-    stored = lax.broadcasted_iota(I32, (slab_rows, LANES), 0) + me * slab_rows
+    stored = lax.broadcasted_iota(I32, (slab_rows, LANES), 0) + mesh_me * slab_rows
     picked = jnp.zeros((slab_rows, LANES), I32)
     for b in range(home_ref.shape[0]):
         hit = home_ref[b : b + 1, :] == stored
@@ -114,6 +133,14 @@
             jnp.where(high, table, 0.0), axis=0, keepdims=True
         ).astype(I32)
 
+    def wait_query(d, carry):
+        p = plane * half + lax.rem(spot + d, half)
+        query_copy(p, p, device_of(p)[1]).wait_recv()
+        return carry
+
+    lax.fori_loop(1, half, wait_query, 0)
+    plane_copy(plane).start()
+
     def wait_load(c, carry):
         load(c).wait()
         return carry
@@ -121,24 +148,17 @@
     lax.fori_loop(0, chunks, wait_load, 0)
 
     columns = tile * tokens
-    tiles = shards // tile
+    tiles = half // tile
     group = lax.broadcasted_iota(I32, (tile, columns), 0)
     member = lax.broadcasted_iota(I32, (tile, columns), 1) // tokens
     adder = jnp.where(group == member, 1.0, 0.0).astype(BF16)
 
     def one_tile(b, carry):
-        t = lax.rem(me // tile + b, tiles)
-
-        def wait_query(i, c):
-            p = t * tile + i
-
-            @pl.when(p != me)
-            def _():
-                query_copy(p, p, {"query": lax.axis_index("query")}).wait_recv()
-
-            return c
-
-        lax.fori_loop(0, tile, wait_query, 0)
+        @pl.when(b == tiles)
+        def _():
+            plane_copy(1 - plane).wait_recv()
+
+        t = lax.rem(plane * tiles + b, 2 * tiles)
         query_t[...] = qbuf[pl.ds(t * tile, tile)].reshape(columns, width).T
 
         for r in range(0, slab_rows, band):
@@ -175,20 +195,19 @@
 
             @pl.when(p != me)
             def _():
-                device = {"corpus": p // inner, "query": lax.rem(p, inner)}
-                score_copy(p, me, device).start()
+                score_copy(p, mesh_me, device_of(p)[1]).start()
 
             @pl.when(p == me)
             def _():
-                got[pl.ds(p, 1)] = scores[i : i + 1].reshape(1, 1, slab_rows)
-
-        return carry
-
-    lax.fori_loop(0, tiles, one_tile, 0)
+                got[pl.ds(mesh_me, 1)] = scores[i : i + 1].reshape(1, 1, slab_rows)
+
+        return carry
+
+    lax.fori_loop(0, 2 * tiles, one_tile, 0)
 
     def wait_scores(d, carry):
-        p, device = peer(d)
-        score_copy(p, p, device).wait_recv()
+        p, slot, device = peer(d)
+        score_copy(p, slot, device).wait_recv()
         return carry
 
     lax.fori_loop(1, shards, wait_scores, 0)
@@ -215,12 +234,19 @@
     out_ref[...] = ranked[:, : out_ref.shape[1]]
 
     def wait_sends(d, carry):
-        p, device = peer(d)
-        query_copy(p, p, device).wait_send()
-        score_copy(p, p, device).wait_send()
+        p, slot, device = peer(d)
+        score_copy(p, slot, device).wait_send()
         return carry
 
     lax.fori_loop(1, shards, wait_sends, 0)
+
+    def wait_queries(d, carry):
+        p = plane * half + lax.rem(spot + d, half)
+        query_copy(p, p, device_of(p)[1]).wait_send()
+        return carry
+
+    lax.fori_loop(1, half, wait_queries, 0)
+    plane_copy(plane).wait_send()
 
 
 def on_device(queries, passages, token_lengths, candidates, passage_home):
@@ -230,7 +256,7 @@
     tokens = queries.shape[1]
     count = candidates.shape[1]
     tile = max(1, COLUMNS // tokens)
-    while shards % tile:
+    while (shards // 2) % tile:
         tile -= 1
     chunk = next(c for c in range(CHUNK, 0, -1) if slots % c == 0)
     band = BAND if slab_rows % BAND == 0 else slab_rows
@@ -257,6 +283,8 @@
             pltpu.SemaphoreType.DMA((slots // chunk,)),
             pltpu.SemaphoreType.DMA((shards,)),
             pltpu.SemaphoreType.DMA((shards,)),
+            pltpu.SemaphoreType.DMA,
+            pltpu.SemaphoreType.DMA,
             pltpu.SemaphoreType.DMA((shards,)),
             pltpu.SemaphoreType.DMA((shards,)),
         ],

time: 26.6 us -> 26.5 us (level)
  the two profiles are of different devices: /device:TPU:0 before, /device:TPU:1 now
where the time goes in v3:
time: 26.5 us; the launch traced here: 26.4 us
  Pallas kernels  25.2 us (95%)
  local copies, waits for them, and re-layouts  1.19 us (4%)
    pallas_call x1, Pallas kernels, on_device(): pl.pallas_call(functools.partial(kernel, shards, inner, tile, chunk, band...  25.2 us
    unnamed x1, local copies, waits for them, and re-layouts  1.19 us

profile of v3, /device:TPU:1, one launch (start us, length us, event | category | flops | bytes accessed | tf_op | source)
XLA Modules:
  0.0 26.4 jit_solution(3128234989373942048)
XLA Ops:
  0.0 25.2 %shard_map.55 = f32[1,100]{1,0:T(1,128)} custom-call(bf16[1,32,128]{2,1,0:T(8,128)(2,1)} %q_ref.1, bf16[180,128,128]{2,1,0:T(8,128)(2,1)} %bitcast.3, s32[16,128]{1,0:T(8,128)} %bitcast.4, s32[1,256]{1,0:T(1,128)} %cand_hbm.1, s32[16,128]{1,0:T(8,128)} %bitcast.5), custom_call_target="tpu_custom_call" | custom-call | tf_op jit(solution)/shard_map/pallas_call | solution.py:265
  25.2 1.2 %copy.7 = f32[1,100]{1,0:T(1,128)} copy(f32[1,100]{1,0:T(1,128)} %shard_map.55) | data formatting | bytes 800

commit v4 on v3

--- a/solution.py
+++ b/solution.py
@@ -81,7 +81,7 @@
 
     def query_copy(slot, sem_s, device):
         return pltpu.make_async_remote_copy(
-            src_ref=q_ref, dst_ref=qbuf.at[pl.ds(slot, 1)],
+            src_ref=qbuf.at[pl.ds(me, 1)], dst_ref=qbuf.at[pl.ds(slot, 1)],
             send_sem=qs_sem.at[sem_s], recv_sem=qr_sem.at[slot],
             device_id=device, device_id_type=MESH,
         )
@@ -106,8 +106,9 @@
         query_copy(me, p, device_of(p)[1]).start()
         return carry
 
+    small[3].wait()
     lax.fori_loop(1, half, send_query, 0)
-    for copy in small:
+    for copy in small[:3]:
         copy.wait()
 
     stored = lax.broadcasted_iota(I32, (slab_rows, LANES), 0) + mesh_me * slab_rows
@@ -141,12 +142,6 @@
     lax.fori_loop(1, half, wait_query, 0)
     plane_copy(plane).start()
 
-    def wait_load(c, carry):
-        load(c).wait()
-        return carry
-
-    lax.fori_loop(0, chunks, wait_load, 0)
-
     columns = tile * tokens
     tiles = half // tile
     group = lax.broadcasted_iota(I32, (tile, columns), 0)
@@ -165,6 +160,12 @@
             live = lens[r : r + band, :]
 
             def some_slots(g, top):
+                if r == 0:
+
+                    @pl.when(b == 0)
+                    def _():
+                        load(g).wait()
+
                 block = slab[pl.ds(g * chunk, chunk), r : r + band, :]
                 similar = jnp.dot(
                     block.reshape(chunk * band, width), query_t[...],

time: 26.5 us -> 26.5 us (level)
  no operation moved by 1% of the time
where the time goes in v4:
time: 26.5 us; the launch traced here: 26.3 us
  Pallas kernels  25.1 us (95%)
  local copies, waits for them, and re-layouts  1.19 us (4%)
    pallas_call x1, Pallas kernels, on_device(): pl.pallas_call(functools.partial(kernel, shards, inner, tile, chunk, band...  25.1 us
    unnamed x1, local copies, waits for them, and re-layouts  1.19 us

profile of v4, /device:TPU:1, one launch (start us, length us, event | category | flops | bytes accessed | tf_op | source)
XLA Modules:
  0.0 26.3 jit_solution(10635155133619177982)
XLA Ops:
  0.0 25.1 %shard_map.55 = f32[1,100]{1,0:T(1,128)} custom-call(bf16[1,32,128]{2,1,0:T(8,128)(2,1)} %q_ref.1, bf16[180,128,128]{2,1,0:T(8,128)(2,1)} %bitcast.3, s32[16,128]{1,0:T(8,128)} %bitcast.4, s32[1,256]{1,0:T(1,128)} %cand_hbm.1, s32[16,128]{1,0:T(8,128)} %bitcast.5), custom_call_target="tpu_custom_call" | custom-call | tf_op jit(solution)/shard_map/pallas_call | solution.py:266
  25.1 1.2 %copy.7 = f32[1,100]{1,0:T(1,128)} copy(f32[1,100]{1,0:T(1,128)} %shard_map.55) | data formatting | bytes 800

commit v5 on v4

--- a/solution.py
+++ b/solution.py
@@ -61,7 +61,7 @@
         pl.semaphore_signal(barrier, inc=1, device_id=peer(d)[2], device_id_type=MESH)
         return carry
 
-    lax.fori_loop(1, shards, greet, 0)
+    lax.fori_loop(1, shards, greet, 0, unroll=True)
     small = [
         pltpu.make_async_copy(src, dst, small_sem.at[k])
         for k, (src, dst) in enumerate(
@@ -77,39 +77,8 @@
         copy.start()
     for c in range(chunks):
         load(c).start()
-    pl.semaphore_wait(barrier, shards - 1)
-
-    def query_copy(slot, sem_s, device):
-        return pltpu.make_async_remote_copy(
-            src_ref=qbuf.at[pl.ds(me, 1)], dst_ref=qbuf.at[pl.ds(slot, 1)],
-            send_sem=qs_sem.at[sem_s], recv_sem=qr_sem.at[slot],
-            device_id=device, device_id_type=MESH,
-        )
-
-    def score_copy(row, slot, device):
-        return pltpu.make_async_remote_copy(
-            src_ref=sent.at[row], dst_ref=got.at[slot],
-            send_sem=ss_sem.at[row], recv_sem=sr_sem.at[slot],
-            device_id=device, device_id_type=MESH,
-        )
-
-    def plane_copy(which):
-        part = pl.ds(which * half, half)
-        return pltpu.make_async_remote_copy(
-            src_ref=qbuf.at[part], dst_ref=qbuf.at[part],
-            send_sem=ps_sem, recv_sem=pr_sem,
-            device_id=device_of((1 - plane) * half + spot)[1], device_id_type=MESH,
-        )
-
-    def send_query(d, carry):
-        p = plane * half + lax.rem(spot + d, half)
-        query_copy(me, p, device_of(p)[1]).start()
-        return carry
-
-    small[3].wait()
-    lax.fori_loop(1, half, send_query, 0)
-    for copy in small[:3]:
-        copy.wait()
+    small[0].wait()
+    small[1].wait()
 
     stored = lax.broadcasted_iota(I32, (slab_rows, LANES), 0) + mesh_me * slab_rows
     picked = jnp.zeros((slab_rows, LANES), I32)
@@ -120,6 +89,38 @@
     lens[...] = jnp.dot(
         picked.astype(F32).astype(BF16), ones, preferred_element_type=F32
     ).astype(I32)
+    small[2].wait()
+    small[3].wait()
+    pl.semaphore_wait(barrier, shards - 1)
+
+    def query_copy(slot, sem_s, device):
+        return pltpu.make_async_remote_copy(
+            src_ref=qbuf.at[pl.ds(me, 1)], dst_ref=qbuf.at[pl.ds(slot, 1)],
+            send_sem=qs_sem.at[sem_s], recv_sem=qr_sem.at[slot],
+            device_id=device, device_id_type=MESH,
+        )
+
+    def score_copy(row, slot, device):
+        return pltpu.make_async_remote_copy(
+            src_ref=sent.at[row], dst_ref=got.at[slot],
+            send_sem=ss_sem.at[row], recv_sem=sr_sem.at[slot],
+            device_id=device, device_id_type=MESH,
+        )
+
+    def plane_copy(which):
+        part = pl.ds(which * half, half)
+        return pltpu.make_async_remote_copy(
+            src_ref=qbuf.at[part], dst_ref=qbuf.at[part],
+            send_sem=ps_sem, recv_sem=pr_sem,
+            device_id=device_of((1 - plane) * half + spot)[1], device_id_type=MESH,
+        )
+
+    def send_query(d, carry):
+        p = plane * half + lax.rem(spot + d, half)
+        query_copy(me, p, device_of(p)[1]).start()
+        return carry
+
+    lax.fori_loop(1, half, send_query, 0, unroll=True)
 
     count = cand_ref.shape[1]
     cand = cand_ref[...]
@@ -139,7 +140,7 @@
         query_copy(p, p, device_of(p)[1]).wait_recv()
         return carry
 
-    lax.fori_loop(1, half, wait_query, 0)
+    lax.fori_loop(1, half, wait_query, 0, unroll=True)
     plane_copy(plane).start()
 
     columns = tile * tokens
@@ -211,7 +212,7 @@
         score_copy(p, slot, device).wait_recv()
         return carry
 
-    lax.fori_loop(1, shards, wait_scores, 0)
+    lax.fori_loop(1, shards, wait_scores, 0, unroll=True)
     table = got[...].reshape(shards, slab_rows)
     offset = lax.broadcasted_iota(I32, (slab_rows, count), 0) == where_row[1:2, :]
     offset = jnp.where(offset, 1.0, 0.0).astype(BF16)
@@ -239,14 +240,14 @@
         score_copy(p, slot, device).wait_send()
         return carry
 
-    lax.fori_loop(1, shards, wait_sends, 0)
+    lax.fori_loop(1, shards, wait_sends, 0, unroll=True)
 
     def wait_queries(d, carry):
         p = plane * half + lax.rem(spot + d, half)
         query_copy(p, p, device_of(p)[1]).wait_send()
         return carry
 
-    lax.fori_loop(1, half, wait_queries, 0)
+    lax.fori_loop(1, half, wait_queries, 0, unroll=True)
     plane_copy(plane).wait_send()
 
 

time: 26.5 us -> 26.3 us (level)
  no operation moved by 1% of the time
where the time goes in v5:
time: 26.3 us; the launch traced here: 26.1 us
  Pallas kernels  24.9 us (95%)
  local copies, waits for them, and re-layouts  1.19 us (5%)
    pallas_call x1, Pallas kernels, on_device(): pl.pallas_call(functools.partial(kernel, shards, inner, tile, chunk, band...  24.9 us
    unnamed x1, local copies, waits for them, and re-layouts  1.19 us

profile of v5, /device:TPU:1, one launch (start us, length us, event | category | flops | bytes accessed | tf_op | source)
XLA Modules:
  0.0 26.1 jit_solution(16645306178319188641)
XLA Ops:
  0.0 24.9 %shard_map.55 = f32[1,100]{1,0:T(1,128)} custom-call(bf16[1,32,128]{2,1,0:T(8,128)(2,1)} %q_ref.1, bf16[180,128,128]{2,1,0:T(8,128)(2,1)} %bitcast.3, s32[16,128]{1,0:T(8,128)} %bitcast.4, s32[1,256]{1,0:T(1,128)} %cand_hbm.1, s32[16,128]{1,0:T(8,128)} %bitcast.5), custom_call_target="tpu_custom_call" | custom-call | tf_op jit(solution)/shard_map/pallas_call | solution.py:267
  24.9 1.2 %copy.7 = f32[1,100]{1,0:T(1,128)} copy(f32[1,100]{1,0:T(1,128)} %shard_map.55) | data formatting | bytes 800
